TPU v7x, 128 devices: a whole 4x4x4 slice. The times are simulated.
128 devices in a mesh: blk: 128 (over x, y, z, core).
Axes of the slice: x: 4, y: 4, z: 4, core: 2. Of those that a mesh axis runs over, the one named last changes fastest.
Arguments:
- tokens: bfloat16 [16384, 768], P('blk'), may hold values from -6 to 6
- store_keys: bfloat16 [8192, 768], P('blk'), may hold values from -9 to 9
- store_values: bfloat16 [8192, 768], P('blk'), may hold values from -6 to 6
- retrieved: int32 [16384, 1024], P('blk'), may hold values from 0 to 8191, as said below
- seq_lengths: int32 [128], P('blk'), may hold values from 64 to 128, as said below
- w_query: bfloat16 [768, 768], replicated, may hold values from -0.21875 to 0.21875
- w_key: bfloat16 [768, 768], replicated, may hold values from -0.4375 to 0.4375
- w_value: bfloat16 [768, 768], replicated, may hold values from -0.21875 to 0.21875
- w_out: bfloat16 [768, 768], replicated, may hold values from -0.875 to 0.875
- c_query: bfloat16 [768, 768], replicated, may hold values from -0.21875 to 0.21875
- c_out: bfloat16 [768, 768], replicated, may hold values from -0.875 to 0.875
- ffn_in: bfloat16 [768, 3072], replicated, may hold values from -0.21875 to 0.21875
- ffn_bias: float32 [3072], replicated, may hold values from -3 to 3
- ffn_out: bfloat16 [3072, 768], replicated, may hold values from -0.109375 to 0.109375
- gain_self: float32 [768], replicated, may hold values from 0.5 to 1.5
- shift_self: float32 [768], replicated, may hold values from -2 to 2
- gain_cross: float32 [768], replicated, may hold values from 0.5 to 1.5
- shift_cross: float32 [768], replicated, may hold values from -2 to 2
- gain_ffn: float32 [768], replicated, may hold values from 0.5 to 1.5
- shift_ffn: float32 [768], replicated, may hold values from -2 to 2
- cotangent: float32 [16384, 768], P('blk'), may hold values from -24 to 24
Outputs:
- block_output: float32 [16384, 768], P('blk')
- d_tokens: float32 [16384, 768], P('blk')
- d_store_keys: float32 [8192, 768], P('blk')
- d_store_values: float32 [8192, 768], P('blk')
- d_w_query: float32 [768, 768], P('blk')
- d_w_key: float32 [768, 768], P('blk')
- d_w_value: float32 [768, 768], P('blk')
- d_w_out: float32 [768, 768], P('blk')
- d_c_query: float32 [768, 768], P('blk')
- d_c_out: float32 [768, 768], P('blk')
- d_ffn_in: float32 [768, 3072], P('blk')
- d_ffn_bias: float32 [3072], P('blk')
- d_ffn_out: float32 [3072, 768], P('blk')
- d_gain_self: float32 [768], P('blk')
- d_shift_self: float32 [768], P('blk')
- d_gain_cross: float32 [768], P('blk')
- d_shift_cross: float32 [768], P('blk')
- d_gain_ffn: float32 [768], P('blk')
- d_shift_ffn: float32 [768], P('blk')
Inputs may be any that keep to these rules, and one draw needn't show every extreme that they name: `retrieved`: each row names 1024 different datastore rows. `seq_lengths`: positions from a sequence's length on are padding; some sequence has none.
All inputs are finite; a program needn't handle non-finite values.
Results may differ from a plain program's by a relative error of at most 0.035.
Values may be sent and summed in bfloat16 or wider, within the bound.
No kernel may reach another device: no remote copies, remote signals or barrier semaphores. Data moves between devices by JAX's collectives and lax.ppermute only.
A program may use at most 320 MiB of HBM per device.

v0:
```python
from functools import partial
import math

import jax
import jax.numpy as jnp
from jax import lax
from jax.sharding import PartitionSpec as P

HEADS = 12
HEAD_DIM = 64


def as_low(operand):
    return operand.astype(jnp.bfloat16)


def product(operand_one, operand_two):
    return jnp.dot(operand_one, operand_two, preferred_element_type=jnp.float32)


def product_tn(operand_one, operand_two):
    return lax.dot_general(
        operand_one, operand_two, (((0,), (0,)), ((), ())), preferred_element_type=jnp.float32
    )


def product_nt(operand_one, operand_two):
    return lax.dot_general(
        operand_one, operand_two, (((1,), (1,)), ((), ())), preferred_element_type=jnp.float32
    )


def layer_norm(summed, norm_gain, norm_shift):
    average = jnp.mean(summed, -1, keepdims=True)
    centred = summed - average
    spread = lax.rsqrt(jnp.mean(centred * centred, -1, keepdims=True) + 1e-05)
    normed = centred * spread
    return (normed * norm_gain + norm_shift, normed, spread)


def norm_back(upstream, normed, spread, norm_gain):
    scaled = upstream * norm_gain
    centred_grad = spread * (
        scaled
        - jnp.mean(scaled, -1, keepdims=True)
        - normed * jnp.mean(scaled * normed, -1, keepdims=True)
    )
    return (centred_grad, jnp.sum(upstream * normed, 0), jnp.sum(upstream, 0))


def shards(
    tokens,
    store_keys,
    store_values,
    retrieved,
    seq_lengths,
    w_query,
    w_key,
    w_value,
    w_out,
    c_query,
    c_out,
    ffn_in,
    ffn_bias,
    ffn_out,
    gain_self,
    shift_self,
    gain_cross,
    shift_cross,
    gain_ffn,
    shift_ffn,
    cotangent,
):
    rows_here = tokens.shape[0]
    model_width = tokens.shape[1]
    scaling = HEAD_DIM ** (-0.5)
    head_shape = (rows_here, HEADS, HEAD_DIM)
    queries = as_low(product(tokens, w_query)).reshape(head_shape)
    keys_self = as_low(product(tokens, w_key)).reshape(head_shape)
    values_self = as_low(product(tokens, w_value)).reshape(head_shape)
    position = jnp.arange(rows_here)
    allowed = (position[None, :] <= position[:, None]) & (position[None, :] < seq_lengths[0])
    raw_scores = jnp.einsum("qhd,khd->hqk", queries, keys_self, preferred_element_type=jnp.float32)
    scores = jnp.where(allowed[None], raw_scores * scaling, -1e30)
    shifted = jnp.exp(scores - jnp.max(scores, -1, keepdims=True))
    weights_self = shifted / jnp.sum(shifted, -1, keepdims=True)
    low_weights = as_low(weights_self)
    attended_full = jnp.einsum(
        "hqk,khd->qhd", low_weights, values_self, preferred_element_type=jnp.float32
    )
    attended = as_low(attended_full).reshape(rows_here, model_width)
    hidden_one, normed_one, spread_one = layer_norm(
        tokens.astype(jnp.float32) + product(attended, w_out), gain_self, shift_self
    )
    low_one = as_low(hidden_one)
    cross_queries = as_low(product(low_one, c_query)).reshape(head_shape)
    gathered_keys, gathered_values = (
        lax.all_gather(store_keys, "blk", axis=0, tiled=True),
        lax.all_gather(store_values, "blk", axis=0, tiled=True),
    )
    store_total = gathered_keys.shape[0]
    shard_rows = store_keys.shape[0]
    group_size = math.gcd(16, store_total // shard_rows)
    block_rows = shard_rows * group_size
    blocks = store_total // block_rows
    hit_mask = (
        jnp.zeros((rows_here, store_total), jnp.bool_).at[position[:, None], retrieved].set(True)
    )

    def cross_scores(number, keys_all):
        first_row = number * block_rows
        key_block = keys_all[first_row : first_row + block_rows].reshape(
            block_rows, HEADS, HEAD_DIM
        )
        raw_block = jnp.einsum(
            "qhd,khd->hqk", cross_queries, key_block, preferred_element_type=jnp.float32
        )
        mask_block = hit_mask[:, first_row : first_row + block_rows]
        return (jnp.where(mask_block[None], raw_block * scaling, -1e30), key_block)

    running_max = jnp.full((HEADS, rows_here), -1e30, jnp.float32)
    running_sum = jnp.zeros((HEADS, rows_here), jnp.float32)
    for number in range(blocks):
        scores_block, unused_keys = cross_scores(number, gathered_keys)
        new_max = jnp.maximum(running_max, jnp.max(scores_block, -1))
        running_sum = running_sum * jnp.exp(running_max - new_max) + jnp.sum(
            jnp.exp(scores_block - new_max[..., None]), -1
        )
        running_max = new_max
    log_total = running_max + jnp.log(running_sum)
    cross_full = jnp.zeros(head_shape, jnp.float32)
    for number in range(blocks):
        scores_block, unused_keys = cross_scores(number, gathered_keys)
        probs_block = jnp.exp(scores_block - log_total[..., None])
        first_row = number * block_rows
        value_block = gathered_values[first_row : first_row + block_rows].reshape(
            block_rows, HEADS, HEAD_DIM
        )
        cross_full = cross_full + jnp.einsum(
            "hqk,khd->qhd", as_low(probs_block), value_block, preferred_element_type=jnp.float32
        )
    cross_out = as_low(cross_full).reshape(rows_here, model_width)
    hidden_two, normed_two, spread_two = layer_norm(
        hidden_one + product(cross_out, c_out), gain_cross, shift_cross
    )
    low_two = as_low(hidden_two)
    pre_act = product(low_two, ffn_in) + ffn_bias
    activated, gelu_back = jax.vjp(partial(jax.nn.gelu, approximate=False), pre_act)
    low_act = as_low(activated)
    block_output, normed_three, spread_three = layer_norm(
        hidden_two + product(low_act, ffn_out), gain_ffn, shift_ffn
    )
    grad_three, d_gain_ffn, d_shift_ffn = norm_back(cotangent, normed_three, spread_three, gain_ffn)
    grad_ffn = as_low(grad_three)
    d_ffn_out = product_tn(low_act, grad_ffn)
    grad_pre = gelu_back(product_nt(grad_ffn, ffn_out))[0]
    low_pre = as_low(grad_pre)
    d_ffn_bias = jnp.sum(low_pre.astype(jnp.float32), 0)
    d_ffn_in = product_tn(low_two, low_pre)
    grad_two_in = grad_three + product_nt(low_pre, ffn_in)
    grad_two, d_gain_cross, d_shift_cross = norm_back(
        grad_two_in, normed_two, spread_two, gain_cross
    )
    grad_cross = as_low(grad_two)
    d_c_out = product_tn(cross_out, grad_cross)
    grad_attn = as_low(product_nt(grad_cross, c_out)).reshape(head_shape)
    row_terms = jnp.sum(grad_attn.astype(jnp.float32) * cross_full, -1).T
    keys_back, values_back = (gathered_keys, gathered_values)
    grad_queries = jnp.zeros(head_shape, jnp.float32)
    key_terms = []
    value_terms = []
    for number in range(blocks):
        scores_block, key_block = cross_scores(number, keys_back)
        probs_block = jnp.exp(scores_block - log_total[..., None])
        first_row = number * block_rows
        value_block = values_back[first_row : first_row + block_rows].reshape(
            block_rows, HEADS, HEAD_DIM
        )
        grad_probs = jnp.einsum(
            "qhd,khd->hqk", grad_attn, value_block, preferred_element_type=jnp.float32
        )
        grad_scores = as_low(probs_block * (grad_probs - row_terms[..., None]) * scaling)
        grad_queries = grad_queries + jnp.einsum(
            "hqk,khd->qhd", grad_scores, key_block, preferred_element_type=jnp.float32
        )
        key_terms.append(
            jnp.einsum(
                "hqk,qhd->khd", grad_scores, cross_queries, preferred_element_type=jnp.float32
            ).reshape(block_rows, model_width)
        )
        value_terms.append(
            jnp.einsum(
                "hqk,qhd->khd", as_low(probs_block), grad_attn, preferred_element_type=jnp.float32
            ).reshape(block_rows, model_width)
        )
    d_store_keys, d_store_values = (
        lax.psum_scatter(jnp.concatenate(key_terms, 0), "blk", scatter_dimension=0, tiled=True),
        lax.psum_scatter(jnp.concatenate(value_terms, 0), "blk", scatter_dimension=0, tiled=True),
    )
    low_cquery = as_low(grad_queries.reshape(rows_here, model_width))
    d_c_query = product_tn(low_one, low_cquery)
    grad_one_in = grad_two + product_nt(low_cquery, c_query)
    grad_one, d_gain_self, d_shift_self = norm_back(grad_one_in, normed_one, spread_one, gain_self)
    grad_out = as_low(grad_one)
    d_w_out = product_tn(attended, grad_out)
    grad_self = as_low(product_nt(grad_out, w_out)).reshape(head_shape)
    self_terms = jnp.sum(grad_self.astype(jnp.float32) * attended_full, -1).T
    grad_weights = jnp.einsum(
        "qhd,khd->hqk", grad_self, values_self, preferred_element_type=jnp.float32
    )
    grad_raw = as_low(weights_self * (grad_weights - self_terms[..., None]) * scaling)
    grad_query = as_low(
        jnp.einsum("hqk,khd->qhd", grad_raw, keys_self, preferred_element_type=jnp.float32).reshape(
            rows_here, model_width
        )
    )
    grad_key = as_low(
        jnp.einsum("hqk,qhd->khd", grad_raw, queries, preferred_element_type=jnp.float32).reshape(
            rows_here, model_width
        )
    )
    grad_value = as_low(
        jnp.einsum(
            "hqk,qhd->khd", low_weights, grad_self, preferred_element_type=jnp.float32
        ).reshape(rows_here, model_width)
    )
    d_tokens = (
        grad_one
        + product_nt(grad_query, w_query)
        + product_nt(grad_key, w_key)
        + product_nt(grad_value, w_value)
    )
    d_w_query = product_tn(tokens, grad_query)
    d_w_key = product_tn(tokens, grad_key)
    d_w_value = product_tn(tokens, grad_value)
    reduced = (
        lax.psum_scatter(d_w_query, "blk", scatter_dimension=0, tiled=True),
        lax.psum_scatter(d_w_key, "blk", scatter_dimension=0, tiled=True),
        lax.psum_scatter(d_w_value, "blk", scatter_dimension=0, tiled=True),
        lax.psum_scatter(d_w_out, "blk", scatter_dimension=0, tiled=True),
        lax.psum_scatter(d_c_query, "blk", scatter_dimension=0, tiled=True),
        lax.psum_scatter(d_c_out, "blk", scatter_dimension=0, tiled=True),
        lax.psum_scatter(d_ffn_in, "blk", scatter_dimension=0, tiled=True),
        lax.psum_scatter(d_ffn_bias, "blk", scatter_dimension=0, tiled=True),
        lax.psum_scatter(d_ffn_out, "blk", scatter_dimension=0, tiled=True),
        lax.psum_scatter(d_gain_self, "blk", scatter_dimension=0, tiled=True),
        lax.psum_scatter(d_shift_self, "blk", scatter_dimension=0, tiled=True),
        lax.psum_scatter(d_gain_cross, "blk", scatter_dimension=0, tiled=True),
        lax.psum_scatter(d_shift_cross, "blk", scatter_dimension=0, tiled=True),
        lax.psum_scatter(d_gain_ffn, "blk", scatter_dimension=0, tiled=True),
        lax.psum_scatter(d_shift_ffn, "blk", scatter_dimension=0, tiled=True),
    )
    return (
        block_output,
        d_tokens,
        d_store_keys,
        d_store_values,
        reduced[0],
        reduced[1],
        reduced[2],
        reduced[3],
        reduced[4],
        reduced[5],
        reduced[6],
        reduced[7],
        reduced[8],
        reduced[9],
        reduced[10],
        reduced[11],
        reduced[12],
        reduced[13],
        reduced[14],
    )


def solution(mesh):
    return jax.shard_map(
        shards,
        mesh=mesh,
        in_specs=(
            P("blk", None),
            P("blk", None),
            P("blk", None),
            P("blk", None),
            P("blk"),
            P(),
            P(),
            P(),
            P(),
            P(),
            P(),
            P(),
            P(),
            P(),
            P(),
            P(),
            P(),
            P(),
            P(),
            P(),
            P("blk", None),
        ),
        out_specs=(
            P("blk", None),
            P("blk", None),
            P("blk", None),
            P("blk", None),
            P("blk", None),
            P("blk", None),
            P("blk", None),
            P("blk", None),
            P("blk", None),
            P("blk", None),
            P("blk", None),
            P("blk"),
            P("blk", None),
            P("blk"),
            P("blk"),
            P("blk"),
            P("blk"),
            P("blk"),
            P("blk"),
        ),
        check_vma=False,
    )
```

profile of v0, /device:TPU:8, one launch (start us, length us, event | category | flops | bytes accessed | tf_op | source)
XLA Modules:
  0.0 1939.8 jit_solution(5440798165733215860)
XLA Ops:
  16.4 545.1 %scatter_custom_fusion = pred[1048576]{0:T(1024)(128)(4,1)S(1)} fusion(s32[131072]{0:T(1024)S(1)} %bitcast.368, pred[131072]{0:T(1024)(128)(4,1)S(1)} %broadcast.203, pred[]{:T(512)} %constant.13.clone.1), kind=kCustom, calls=%fused_computation.52 | custom fusion | bytes 1048577
  571.2 9.5 fusion.128
  583.4 9.3 fusion.127
  669.2 6.4 exponential_reduce_fusion.4
  679.6 6.0 convolution_add_fusion.22
  685.6 6.0 convolution_add_fusion.21
  723.3 6.5 multiply_convert_fusion.6
  745.8 6.0 multiply_convert_fusion.1
  791.5 6.2 fusion.72
  801.6 6.4 fusion.69
  811.7 6.5 fusion.66
  821.9 6.5 fusion.63
  831.9 6.2 fusion.60
  841.8 6.3 fusion.57
  851.7 6.3 fusion.54
  861.7 6.3 fusion.75
  994.7 345.6 %fusion.123 = (f32[8,768]{1,0:T(8,128)S(1)}, f32[8,768]{1,0:T(8,128)S(1)}, f32[8,768]{1,0:T(8,128)S(1)}, f32[8,3072]{1,0:T(8,128)}) fusion(f32[768,768]{1,0:T(8,128)S(1)} %copy-done.51, f32[768,768]{1,0:T(8,128)} %fusion.118, f32[768,768]{1,0:T(8,128)} %fusion.44, f32[768,3072]{1,0:T(8,128)} %fusion.115), kind=kCustom, calls=%all-reduce-scatter.4 | all-reduce-scatter fusion | flops 5505025 | bytes 16687104
  1347.2 14.2 collective-permute-start.28
  1361.4 31.1 %collective-permute-start.27 = (f32[8,768]{1,0:T(8,128)S(1)}, f32[8,768]{1,0:T(8,128)S(1)}, u32[]{:S(2)}, u32[]{:S(2)}) collective-permute-start(f32[8,768]{1,0:T(8,128)S(1)} %get-tuple-element.102), channel_id=1, source_target_pairs={{0,28},{1,29},{2,30},{3,31},{4,32},{5,33},{6,34},{7,35},{8,36},{9,... | collective-permute-start | bytes 73736
  1660.6 65.6 %all-reduce.18 = (f32[3072]{0:T(1024)S(1)}, f32[768]{0:T(1024)S(1)}, f32[768]{0:T(1024)S(1)}, f32[768]{0:T(1024)S(1)}, f32[768]{0:T(1024)S(1)}, /*index=5*/f32[768]{0:T(1024)S(1)}, f32[768]{0:T(1024)S(1)}) all-reduce(f32[3072]{0:T(1024)} %get-tuple-element.173, ...), channel_id=11, replica_groups=mesh['blk'=128] {'blk'}, use_global_device_ids=true, to_apply=%region_43.44.clone | all-reduce | flops 7680 | bytes 61440
  1730.3 26.5 %concatenate.12 = f32[262,768]{1,0:T(8,128)S(1)} concatenate(f32[6,768]{1,0:T(8,128)} %copy-done.158, f32[8,768]{1,0:T(8,128)} %copy-done.159, f32[8,768]{1,0:T(8,128)} %copy-done.160, f32[8,768]{1,0:T(8,128)} %copy-done.161, f32[8,768]{1,0:T(8,128)} %copy-done.162, f32[8,768]{1,0:T(8,128)} %copy-done.163, f32[8,768]{1,0:T(8,128)} %copy-done.164, f32[8,768]{1,0:T(8,128)} %copy-done.165, ...), dimensions={0} | concatenate | bytes 1609728
  1756.8 26.5 %concatenate.13 = f32[262,768]{1,0:T(8,128)S(1)} concatenate(f32[6,768]{1,0:T(8,128)S(1)} %copy-done.157, f32[8,768]{1,0:T(8,128)} %copy-done.191, f32[8,768]{1,0:T(8,128)} %copy-done.192, f32[8,768]{1,0:T(8,128)} %collective-permute-done.60, f32[8,768]{1,0:T(8,128)} %collective-permute-done.59, f32[8,768]{1,0:T(8,128)} %collective-permute-done.58, ...), dimensions={0} | concatenate | bytes 1609728
  1783.3 25.7 %concatenate.14 = f32[262,768]{1,0:T(8,128)S(1)} concatenate(f32[6,768]{1,0:T(8,128)S(1)} %copy-done.155, f32[8,768]{1,0:T(8,128)} %collective-permute-done.94, f32[8,768]{1,0:T(8,128)} %collective-permute-done.93, f32[8,768]{1,0:T(8,128)} %collective-permute-done.92, f32[8,768]{1,0:T(8,128)} %collective-permute-done.91, f32[8,768]{1,0:T(8,128)} %collective-permute-done.90, ...), dimensions={0} | concatenate | bytes 1609728
  1869.7 55.1 %concatenate.15 = f32[262,3072]{1,0:T(8,128)} concatenate(f32[6,3072]{1,0:T(8,128)} %copy-done.126, f32[8,3072]{1,0:T(8,128)} %copy-done.125, f32[8,3072]{1,0:T(8,128)S(1)} %copy-done.128, f32[8,3072]{1,0:T(8,128)S(1)} %copy-done.130, f32[8,3072]{1,0:T(8,128)S(1)} %copy-done.132, f32[8,3072]{1,0:T(8,128)S(1)} %copy-done.134, f32[8,3072]{1,0:T(8,128)S(1)} %copy-done.136, ...), dimensions={0} | concatenate | bytes 6438912
  (947 shorter events, 684.4 us)
Async XLA Ops:
  7.2 564.0 %all-gather.3.cloned.1.call-start = ((), (), s32[]{:S(2)}) async-start(), calls=%async_computation.3 | async-start | bytes 12681216 | tf_op jit(solution)/shard_map/all_gather | solution.py:98
  8.0 575.4 %all-gather.5.cloned.1.call-start = ((), (), s32[]{:S(2)}) async-start(), calls=%async_computation.4 | async-start | bytes 12681216 | tf_op jit(solution)/shard_map/all_gather | solution.py:99
  8.7 1917.6 %all-reduce.23.cloned.1.call-start = ((), (), s32[]{:S(2)}) async-start(), calls=%async_computation.8 | async-start | bytes 14155776
  784.3 1148.3 %reduce-scatter.19.cloned.1.call-start = ((), (), s32[]{:S(2)}) async-start(), calls=%async_computation.7 | async-start | bytes 9510912 | tf_op jit(solution)/shard_map/reduce_scatter | solution.py:245
  790.7 1141.9 %reduce-scatter.17.cloned.1.call-start = ((), (), s32[]{:S(2)}) async-start(), calls=%async_computation.6 | async-start | bytes 25362432 | tf_op jit(solution)/shard_map/reduce_scatter | solution.py:198
  895.7 1036.8 %reduce-scatter.15.cloned.1.call-start = ((), (), s32[]{:S(2)}) async-start(), calls=%async_computation.5 | async-start | bytes 25362432 | tf_op jit(solution)/shard_map/reduce_scatter | solution.py:197
  1343.2 49.3 %collective-permute-start.31 = (f32[6,768]{1,0:T(8,128)S(1)}, f32[6,768]{1,0:T(8,128)S(1)}, u32[]{:S(2)}, u32[]{:S(2)}) collective-permute-start(f32[6,768]{1,0:T(8,128)S(1)} %slice.160), channel_id=1, source_target_pairs={{0,32},{1,33},{2,34},{3,35},{4,36},{5,37},{6,38},{7,39},{8,40},{9,... | collective-permute-start | bytes 55304
  1344.5 49.3 %collective-permute-start.30 = (f32[8,768]{1,0:T(8,128)S(1)}, f32[8,768]{1,0:T(8,128)S(1)}, u32[]{:S(2)}, u32[]{:S(2)}) collective-permute-start(f32[8,768]{1,0:T(8,128)S(1)} %get-tuple-element.102), channel_id=1, source_target_pairs={{0,31},{1,32},{2,33},{3,34},{4,35},{5,36},{6,37},{7,38},{8,39},{9,... | collective-permute-start | bytes 73736
  1345.8 49.4 %collective-permute-start.29 = (f32[8,768]{1,0:T(8,128)S(1)}, f32[8,768]{1,0:T(8,128)S(1)}, u32[]{:S(2)}, u32[]{:S(2)}) collective-permute-start(f32[8,768]{1,0:T(8,128)S(1)} %get-tuple-element.102), channel_id=1, source_target_pairs={{0,30},{1,31},{2,32},{3,33},{4,34},{5,35},{6,36},{7,37},{8,38},{9,... | collective-permute-start | bytes 73736
  1347.2 49.4 %collective-permute-start.28 = (f32[8,768]{1,0:T(8,128)S(1)}, f32[8,768]{1,0:T(8,128)S(1)}, u32[]{:S(2)}, u32[]{:S(2)}) collective-permute-start(f32[8,768]{1,0:T(8,128)S(1)} %get-tuple-element.102), channel_id=1, source_target_pairs={{0,29},{1,30},{2,31},{3,32},{4,33},{5,34},{6,35},{7,36},{8,37},{9,... | collective-permute-start | bytes 73736
  1361.4 36.6 %collective-permute-start.27 = (f32[8,768]{1,0:T(8,128)S(1)}, f32[8,768]{1,0:T(8,128)S(1)}, u32[]{:S(2)}, u32[]{:S(2)}) collective-permute-start(f32[8,768]{1,0:T(8,128)S(1)} %get-tuple-element.102), channel_id=1, source_target_pairs={{0,28},{1,29},{2,30},{3,31},{4,32},{5,33},{6,34},{7,35},{8,36},{9,... | collective-permute-start | bytes 73736
  1576.8 37.3 %collective-permute-start.126 = (f32[8,3072]{1,0:T(8,128)}, f32[8,3072]{1,0:T(8,128)S(1)}, u32[]{:S(2)}, u32[]{:S(2)}) collective-permute-start(f32[8,3072]{1,0:T(8,128)} %get-tuple-element.105), channel_id=1, source_target_pairs={{0,31},{1,32},{2,33},{3,34},{4,35},{5,36},{6,37},{7,38},{8,39},{9,... | collective-permute-start | bytes 294920
  1589.6 23.2 %collective-permute-start.127 = (f32[6,3072]{1,0:T(8,128)S(1)}, f32[6,3072]{1,0:T(8,128)S(1)}, u32[]{:S(2)}, u32[]{:S(2)}) collective-permute-start(f32[6,3072]{1,0:T(8,128)S(1)} %slice.163), channel_id=1, source_target_pairs={{0,32},{1,33},{2,34},{3,35},{4,36},{5,37},{6,38},{7,39},{8,40},{9,... | collective-permute-start | bytes 221192
  1627.1 21.3 %collective-permute-start.117 = (f32[8,3072]{1,0:T(8,128)}, f32[8,3072]{1,0:T(8,128)S(1)}, u32[]{:S(2)}, u32[]{:S(2)}) collective-permute-start(f32[8,3072]{1,0:T(8,128)} %get-tuple-element.105), channel_id=1, source_target_pairs={{0,22},{1,23},{2,24},{3,25},{4,26},{5,27},{6,28},{7,29},{8,30},{9,... | collective-permute-start | bytes 294920
  1631.2 21.3 %collective-permute-start.116 = (f32[8,3072]{1,0:T(8,128)}, f32[8,3072]{1,0:T(8,128)S(1)}, u32[]{:S(2)}, u32[]{:S(2)}) collective-permute-start(f32[8,3072]{1,0:T(8,128)} %get-tuple-element.105), channel_id=1, source_target_pairs={{0,21},{1,22},{2,23},{3,24},{4,25},{5,26},{6,27},{7,28},{8,29},{9,... | collective-permute-start | bytes 294920
  1636.1 172.9 %collective-permute-start.115 = (f32[8,3072]{1,0:T(8,128)}, f32[8,3072]{1,0:T(8,128)S(1)}, u32[]{:S(2)}, u32[]{:S(2)}) collective-permute-start(f32[8,3072]{1,0:T(8,128)} %get-tuple-element.105), channel_id=1, source_target_pairs={{0,20},{1,21},{2,22},{3,23},{4,24},{5,25},{6,26},{7,27},{8,28},{9,... | collective-permute-start | bytes 294920
  1640.7 171.5 %collective-permute-start.114 = (f32[8,3072]{1,0:T(8,128)}, f32[8,3072]{1,0:T(8,128)S(1)}, u32[]{:S(2)}, u32[]{:S(2)}) collective-permute-start(f32[8,3072]{1,0:T(8,128)} %get-tuple-element.105), channel_id=1, source_target_pairs={{0,19},{1,20},{2,21},{3,22},{4,23},{5,24},{6,25},{7,26},{8,27},{9,... | collective-permute-start | bytes 294920
  1644.4 171.8 %collective-permute-start.113 = (f32[8,3072]{1,0:T(8,128)}, f32[8,3072]{1,0:T(8,128)S(1)}, u32[]{:S(2)}, u32[]{:S(2)}) collective-permute-start(f32[8,3072]{1,0:T(8,128)} %get-tuple-element.105), channel_id=1, source_target_pairs={{0,18},{1,19},{2,20},{3,21},{4,22},{5,23},{6,24},{7,25},{8,26},{9,... | collective-permute-start | bytes 294920
  1648.4 170.9 %collective-permute-start.112 = (f32[8,3072]{1,0:T(8,128)}, f32[8,3072]{1,0:T(8,128)}, u32[]{:S(2)}, u32[]{:S(2)}) collective-permute-start(f32[8,3072]{1,0:T(8,128)} %get-tuple-element.105), channel_id=1, source_target_pairs={{0,17},{1,18},{2,19},{3,20},{4,21},{5,22},{6,23},{7,24},{8,25},{9,... | collective-permute-start | bytes 294920
  1652.5 172.5 %collective-permute-start.111 = (f32[8,3072]{1,0:T(8,128)}, f32[8,3072]{1,0:T(8,128)}, u32[]{:S(2)}, u32[]{:S(2)}) collective-permute-start(f32[8,3072]{1,0:T(8,128)} %get-tuple-element.105), channel_id=1, source_target_pairs={{0,16},{1,17},{2,18},{3,19},{4,20},{5,21},{6,22},{7,23},{8,24},{9,... | collective-permute-start | bytes 294920
  1816.2 19.9 %collective-permute-start.108 = (f32[8,3072]{1,0:T(8,128)}, f32[8,3072]{1,0:T(8,128)S(1)}, u32[]{:S(2)}, u32[]{:S(2)}) collective-permute-start(f32[8,3072]{1,0:T(8,128)} %get-tuple-element.105), channel_id=1, source_target_pairs={{0,13},{1,14},{2,15},{3,16},{4,17},{5,18},{6,19},{7,20},{8,21},{9,... | collective-permute-start | bytes 294920
  1819.3 21.2 %collective-permute-start.107 = (f32[8,3072]{1,0:T(8,128)}, f32[8,3072]{1,0:T(8,128)S(1)}, u32[]{:S(2)}, u32[]{:S(2)}) collective-permute-start(f32[8,3072]{1,0:T(8,128)} %get-tuple-element.105), channel_id=1, source_target_pairs={{0,12},{1,13},{2,14},{3,15},{4,16},{5,17},{6,18},{7,19},{8,20},{9,... | collective-permute-start | bytes 294920
  1828.8 20.5 %collective-permute-start.105 = (f32[8,3072]{1,0:T(8,128)}, f32[8,3072]{1,0:T(8,128)S(1)}, u32[]{:S(2)}, u32[]{:S(2)}) collective-permute-start(f32[8,3072]{1,0:T(8,128)} %get-tuple-element.105), channel_id=1, source_target_pairs={{0,10},{1,11},{2,12},{3,13},{4,14},{5,15},{6,16},{7,17},{8,18},{9,... | collective-permute-start | bytes 294920
  1836.1 21.1 %collective-permute-start.103 = (f32[8,3072]{1,0:T(8,128)}, f32[8,3072]{1,0:T(8,128)S(1)}, u32[]{:S(2)}, u32[]{:S(2)}) collective-permute-start(f32[8,3072]{1,0:T(8,128)} %get-tuple-element.105), channel_id=1, source_target_pairs={{0,8},{1,9},{2,10},{3,11},{4,12},{5,13},{6,14},{7,15},{8,16},{9,17... | collective-permute-start | bytes 294920
  (353 other events, 15476.1 us)
Sparse Core Ops, SparseCore 0:
  11.1 75.5 all-gather.2
  89.7 72.7 all-gather.4
  784.4 162.4 all-reduce.22
  953.1 219.2 reduce-scatter.18
  1179.1 252.5 reduce-scatter.16
  1438.3 274.8 reduce-scatter.14
where the time goes:
time: 1960 us; the launch traced here: 1940 us
  local copies, waits for them, and re-layouts  880 us (45%)
  blocking collectives  411 us (21%)
  starting transfers between devices  362 us (18%)
  matrix products  235 us (12%)
  other arithmetic  22.5 us (1%)
  between operations  19.7 us (1%)
    unnamed x528, local copies, waits for them, and re-layouts  752 us
    unnamed x2, blocking collectives  411 us
    unnamed x129, starting transfers between devices  362 us
    dot_general x8, matrix products, shards(): jnp.einsum('hqk,qhd->khd', as_low(probs_block), grad_attn, preferred_elem...  50.7 us
  transfers between devices with their start and end apart: 134, of which 7 were waited for; matrix products, arithmetic and copies ran while one was open for 65% of the time, Pallas kernels for 0%

commit v1 on v0

v1 whole, which is shorter than its diff:
```python
import functools
import math

import jax
import jax.numpy as jnp
from jax import lax
from jax.experimental import pallas as pl
from jax.experimental.pallas import tpu as pltpu
from jax.sharding import Mesh, PartitionSpec as P

F32 = jnp.float32
BF = jnp.bfloat16
LOWEST = -1e30
LOG2E = math.log2(math.e)
SCALE = 64 ** (-0.5)
CHIP = ("x", "y", "z")
ALL = ("x", "y", "z", "c")
ORDERS = (("x", "y", "z"), ("y", "z", "x"), ("z", "x", "y"))


def low(v):
    return v.astype(BF)


def nn(a, b):
    return jnp.dot(a, b, preferred_element_type=F32)


def nt(a, b):
    return lax.dot_general(a, b, (((1,), (1,)), ((), ())), preferred_element_type=F32)


def tn(a, b):
    return lax.dot_general(a, b, (((0,), (0,)), ((), ())), preferred_element_type=F32)


def mask_body(ret_ref, out_ref, m_ref):
    hi_io=lax.broadcasted_iota(jnp.int32,(64,1024),0)
    lo_io=lax.broadcasted_iota(jnp.int32,(128,1024),0)
    def group(g,_):
        idx=ret_ref[pl.ds(pl.multiple_of(g*8,8),8),:]
        hi=idx>>7; lo=idx&127
        for j in range(8):
            hh=jnp.where(hi_io==hi[j:j+1,:],1.0,0.0).astype(BF)
            ll=jnp.where(lo_io==lo[j:j+1,:],1.0,0.0).astype(BF)
            m_ref[g*8+j]=nt(hh,ll)
        return 0
    lax.fori_loop(0,16,group,0)
    def flip(h,_):
        blk=m_ref[:,h,:]
        out_ref[h]=(blk.T-1.0)*(1e30)
        return 0
    lax.fori_loop(0,64,flip,0)

def make_mask(retrieved):
    return pl.pallas_call(mask_body,
        out_shape=jax.ShapeDtypeStruct((64,128,128),F32),
        in_specs=[pl.BlockSpec(memory_space=pltpu.VMEM)],
        out_specs=pl.BlockSpec(memory_space=pltpu.VMEM),
        scratch_shapes=[pltpu.VMEM((128,64,128),F32)],
        compiler_params=pltpu.CompilerParams(vmem_limit_bytes=48*2**20),
        name="mask")(retrieved)

def fwd_body(k_ref,v_ref,b0_ref,b1_ref,ct_ref,x_ref,l_ref,acc,ms,ls,*,sub):
    step=pl.program_id(1)
    @pl.when(step==0)
    def _():
        acc[...]=jnp.zeros_like(acc)
        ms[...]=jnp.full_like(ms,LOWEST)
        ls[...]=jnp.zeros_like(ls)
    nsub=k_ref.shape[0]//sub
    def one(i,_):
        sl=pl.ds(i*sub,sub)
        r=sub*128
        kk=k_ref[sl].reshape(r,128)
        vt=v_ref[sl].reshape(r,128).T
        bias=jnp.concatenate([b0_ref[sl].reshape(r,128),b1_ref[sl].reshape(r,128)],1)
        for h in range(2):
            t=nn(kk,ct_ref[0,h])*(LOG2E*0.125)+bias
            m_old=ms[h]
            m_new=jnp.maximum(m_old,jnp.max(t,0,keepdims=True))
            p=jnp.exp2(t-m_new)
            a=jnp.exp2(m_old-m_new)
            ls[h]=ls[h]*a+jnp.sum(p,0,keepdims=True)
            ms[h]=m_new
            acc[h]=acc[h]*a+nn(vt[h*64:(h+1)*64],p.astype(BF))
        return 0
    lax.fori_loop(0,nsub,one,0)
    @pl.when(step==pl.num_programs(1)-1)
    def _():
        xs=[]
        for h in range(2):
            xs.append(acc[h]/ls[h])
            l_ref[0,h]=ms[h]+jnp.log2(ls[h])
        x_ref[...]=jnp.concatenate(xs,0).T

def cross_fwd(kv,b0,b1,ct,blk=16,sub=4):
    nb=64//blk
    return pl.pallas_call(functools.partial(fwd_body,sub=sub),
        grid=(3,nb),
        in_specs=[pl.BlockSpec((blk,128,128),lambda p,i:(i,0,p)),
                  pl.BlockSpec((blk,128,128),lambda p,i:(i,0,p+3)),
                  pl.BlockSpec((blk,128,128),lambda p,i:(i,0,0)),
                  pl.BlockSpec((blk,128,128),lambda p,i:(i,0,0)),
                  pl.BlockSpec((1,2,128,256),lambda p,i:(p,0,0,0))],
        out_specs=[pl.BlockSpec((256,128),lambda p,i:(0,p)),
                   pl.BlockSpec((1,2,1,256),lambda p,i:(p,0,0,0))],
        out_shape=[jax.ShapeDtypeStruct((256,384),F32),jax.ShapeDtypeStruct((3,2,1,256),F32)],
        scratch_shapes=[pltpu.VMEM((2,64,256),F32),pltpu.VMEM((2,1,256),F32),pltpu.VMEM((2,1,256),F32)],
        compiler_params=pltpu.CompilerParams(vmem_limit_bytes=56*2**20),
        name="cross_fwd")(kv,kv,b0,b1,ct)

def bwd_body(me_ref,k_ref,v_ref,b0_ref,b1_ref,ct_ref,dxt_ref,c_ref,dx_ref,l_ref,dl_ref,o0,o1,o2,o3,dc_ref,*,part):
    d=pl.program_id(0)
    @pl.when(d==0)
    def _():
        dc_ref[...]=jnp.zeros_like(dc_ref)
    def pick(ref,i):
        if part==0: blk=ref[0,i]
        elif part==1: blk=ref[:,0,i]
        else: blk=ref[i,:,0]
        return blk.reshape(512,128)
    outs=(o0,o1,o2,o3)
    for i in range(4):
        kk=pick(k_ref,i); vv=pick(v_ref,i)
        kt=kk.T
        bias=jnp.concatenate([pick(b0_ref,i),pick(b1_ref,i)],1)
        dk=0.;dv=0.
        for h in range(2):
            p=jnp.exp2(nn(kk,ct_ref[h])*(LOG2E*0.125)+bias-l_ref[h])
            dp=nn(vv,dxt_ref[h])-dl_ref[h]
            ds=(p*dp).astype(BF)
            pb=p.astype(BF)
            dv=dv+nn(pb,dx_ref[h])
            dk=dk+nn(ds,c_ref[h])
            dc_ref[h*64:(h+1)*64]+=nn(kt[h*64:(h+1)*64],ds)
        res=jnp.concatenate([dk,dv],1).astype(BF).reshape(4,128,256)
        for j in range(4):
            @pl.when(d==j)
            def _(j=j):
                outs[j][i*4:(i+1)*4]=res

def cross_bwd(me,kv,b0,b1,ct,dxt,c,dx,l,dl,part):
    if part==0:
        shp=(1,4,4); im=lambda d,me:((d+me[0])%4,0,0)
    elif part==1:
        shp=(4,1,4); im=lambda d,me:(0,(d+me[0])%4,0)
    else:
        shp=(4,4,1); im=lambda d,me:(0,0,(d+me[0])%4)
    full=lambda s: pl.BlockSpec(s,lambda d,me:(0,)*len(s))
    sp=lambda col: pl.BlockSpec(shp+(128,128),lambda d,me:im(d,me)+(0,col))
    return pl.pallas_call(functools.partial(bwd_body,part=part),
        grid_spec=pltpu.PrefetchScalarGridSpec(num_scalar_prefetch=1,grid=(4,),
        in_specs=[sp(part),sp(part+3),sp(0),sp(0),full((2,128,256)),full((2,128,256)),full((2,256,128)),full((2,256,128)),full((2,1,256)),full((2,1,256))],
        out_specs=[full((16,128,256))]*4+[full((128,256))]),
        out_shape=[jax.ShapeDtypeStruct((16,128,256),BF)]*4+[jax.ShapeDtypeStruct((128,256),F32)],
        compiler_params=pltpu.CompilerParams(vmem_limit_bytes=56*2**20),
        name="cross_bwd%d"%part)(me,kv,kv,b0,b1,ct,dxt,c,dx,l,dl)


def layer_norm(summed, gain, shift):
    average = jnp.mean(summed, -1, keepdims=True)
    centred = summed - average
    spread = lax.rsqrt(jnp.mean(centred * centred, -1, keepdims=True) + 1e-05)
    normed = centred * spread
    return normed * gain + shift, normed, spread


def norm_back(upstream, normed, spread, gain):
    scaled = upstream * gain
    grad = spread * (
        scaled
        - jnp.mean(scaled, -1, keepdims=True)
        - normed * jnp.mean(scaled * normed, -1, keepdims=True)
    )
    here = slice(0, 256)
    return grad, jnp.sum((upstream * normed)[here], 0), jnp.sum(upstream[here], 0)


def swap(v):
    return lax.ppermute(v, "c", [(0, 1), (1, 0)])


def shift_by(v, axis, d):
    return lax.ppermute(v, axis, [(i, (i + d) % 4) for i in range(4)])


def both(v):
    return jnp.concatenate([v, swap(v)], 0)


def pair_sum(partial):
    other = swap(partial)
    half = partial.shape[0] // 2
    return partial + jnp.concatenate([other[half:], other[:half]], 0)


def scatter_axis(v, dim, axis):
    n = v.shape[dim] // 4
    me = lax.axis_index(axis)
    total = lax.dynamic_slice_in_dim(v, me * n, n, dim).astype(F32)
    for d in (1, 2, 3):
        piece = lax.dynamic_slice_in_dim(v, lax.rem(me + d, 4) * n, n, dim)
        total = total + shift_by(piece, axis, d).astype(F32)
    return total


def scatter_all(v, dim, order):
    for number, axis in enumerate(order):
        v = scatter_axis(v, dim, axis)
        if number < 2:
            v = low(v)
    return v


def head_pad(a):
    six = a.T.reshape(3, 2, 64, 256)
    zero = jnp.zeros_like(six[:, 0])
    return jnp.stack(
        [jnp.concatenate([six[:, 0], zero], 1), jnp.concatenate([zero, six[:, 1]], 1)], 1
    )


def place_matrix(order):
    row = jnp.arange(768)
    chip, unit = row // 12, row % 12
    at = {"x": chip // 16, "y": chip // 4 % 4, "z": chip % 4}
    turned = (at[order[0]] * 4 + at[order[1]]) * 4 + at[order[2]]
    return low((unit * 64 + turned)[:, None] == jnp.arange(768)[None, :])


def shards(
    tokens, store_keys, store_values, retrieved, seq_lengths,
    w_query, w_key, w_value, w_out, c_query, c_out, ffn_in, ffn_bias, ffn_out,
    gain_self, shift_self, gain_cross, shift_cross, gain_ffn, shift_ffn, cotangent,
):
    core = lax.axis_index("c")
    first = core == 0

    def columns(w):
        n = w.shape[1] // 2
        return lax.dynamic_slice_in_dim(w, core * n, n, 1)

    def other_columns(w):
        n = w.shape[1] // 2
        return lax.dynamic_slice_in_dim(w, (1 - core) * n, n, 1)

    def rows(w):
        n = w.shape[0] // 2
        return lax.dynamic_slice_in_dim(w, core * n, n, 0)

    def in_order(mine, other, dim):
        return jnp.where(
            first,
            jnp.concatenate([mine, other], dim),
            jnp.concatenate([other, mine], dim),
        )

    kv_mine = jnp.concatenate([columns(store_keys), columns(store_values)], 1)
    kv_other = swap(jnp.concatenate([other_columns(store_keys), other_columns(store_values)], 1))
    kv_chip = in_order(kv_mine, kv_other, 0)
    kv = lax.all_gather(kv_chip, CHIP, axis=0, tiled=True)

    bias_own = make_mask(retrieved)
    bias_other = swap(bias_own)

    tok = both(tokens)
    cot = both(cotangent)
    lengths = both(seq_lengths)

    def heads(a):
        return a.reshape(2, 128, 6, 64).transpose(0, 2, 1, 3)

    def joined(a):
        return a.transpose(0, 2, 1, 3).reshape(256, 384)

    wq, wk, wv, wo = columns(w_query), columns(w_key), columns(w_value), rows(w_out)
    cq, co = columns(c_query), rows(c_out)
    fi, fb, fo = columns(ffn_in), lax.dynamic_slice_in_dim(ffn_bias, core * 1536, 1536, 0), rows(ffn_out)
    q = heads(low(nn(tok, wq)))
    k = heads(low(nn(tok, wk)))
    v = heads(low(nn(tok, wv)))
    place = jnp.arange(128)
    allowed = (place[None, :] <= place[:, None])[None] & (
        place[None, None, :] < lengths[:, None, None]
    )
    raw = jnp.einsum("bhqd,bhkd->bhqk", q, k, preferred_element_type=F32)
    scores = jnp.where(allowed[:, None], raw * SCALE, LOWEST)
    shifted = jnp.exp(scores - jnp.max(scores, -1, keepdims=True))
    probs = shifted / jnp.sum(shifted, -1, keepdims=True)
    low_probs = low(probs)
    o_full = jnp.einsum("bhqk,bhkd->bhqd", low_probs, v, preferred_element_type=F32)
    o = joined(low(o_full))
    h1, n1, r1 = layer_norm(tok.astype(F32) + pair_sum(nn(o, wo)), gain_self, shift_self)
    low1 = low(h1)
    c = low(nn(low1, cq))
    c_pad = head_pad(c)

    x_full, lse = cross_fwd(kv.reshape(64, 128, 768), bias_own, bias_other, c_pad)
    x = low(x_full)
    h2, n2, r2 = layer_norm(h1 + pair_sum(nn(x, co)), gain_cross, shift_cross)
    low2 = low(h2)
    pre = nn(low2, fi) + fb
    act, gelu_back = jax.vjp(functools.partial(jax.nn.gelu, approximate=False), pre)
    g = low(act)
    out, n3, r3 = layer_norm(h2 + pair_sum(nn(g, fo)), gain_ffn, shift_ffn)

    e3, d_gain_ffn, d_shift_ffn = norm_back(cot, n3, r3, gain_ffn)
    f = low(e3)
    du = low(gelu_back(nt(f, fo))[0])
    d_bias = jnp.sum(du.astype(F32), 0)
    e2, d_gain_cross, d_shift_cross = norm_back(e3 + pair_sum(nt(du, fi)), n2, r2, gain_cross)
    y = low(e2)

    swapped_g = swap(g)
    g_all = in_order(g, jnp.concatenate([swapped_g[128:], swapped_g[:128]], 0), 1)
    swapped_x = swap(x)
    x_all = in_order(x, jnp.concatenate([swapped_x[128:], swapped_x[:128]], 0), 1)
    swapped_o = swap(o)
    o_all = in_order(o, jnp.concatenate([swapped_o[128:], swapped_o[:128]], 0), 1)
    places = [place_matrix(order) for order in ORDERS]

    def placed(a, p):
        return low(nn(a, places[p]))

    def weight_grad(a, b, p):
        return low(tn(placed(a, p), b)).reshape(12, 64, b.shape[1])

    gr_in = scatter_all(weight_grad(low2, du, 0), 1, ORDERS[0])
    gr_out = low(tn(g_all, columns(f))).reshape(4, 4, 4, 48, 384)
    for number, (dim, axis) in enumerate(((1, "y"), (2, "z"), (0, "x"))):
        gr_out = scatter_axis(gr_out, dim, axis)
        gr_out = low(gr_out) if number < 2 else gr_out
    gr_co = scatter_all(weight_grad(x_all, columns(y), 2), 1, ORDERS[2])

    dx = low(nt(y, co))
    delta = SCALE * jnp.sum((dx.astype(F32) * x_full).reshape(256, 6, 64), -1).T.reshape(3, 2, 1, 256)
    dx_pad = head_pad(dx)
    c_rows = c_pad.transpose(0, 1, 3, 2)
    dx_rows = dx_pad.transpose(0, 1, 3, 2)
    dx_scaled = dx_pad * jnp.asarray(SCALE, BF)
    kv6 = kv.reshape(4, 4, 4, 128, 768)
    own6 = bias_own.reshape(4, 4, 4, 128, 128)
    other6 = bias_other.reshape(4, 4, 4, 128, 128)
    dcs, store_grads = [], []
    for p, order in enumerate(ORDERS):
        me = lax.axis_index(order[0]).reshape(1)
        pieces = cross_bwd(
            me, kv6, own6, other6, c_pad[p], dx_scaled[p], c_rows[p], dx_rows[p], lse[p], delta[p], p
        )
        dcs.append(pieces[4])
        total = pieces[0].astype(F32)
        for d in (1, 2, 3):
            total = total + shift_by(pieces[d], order[0], d).astype(F32)
        total = low(total).reshape(4, 4, 128, 256)
        total = low(scatter_axis(total, 0, order[1])[0])
        store_grads.append(scatter_axis(total, 0, order[2])[0])
    dc = low(jnp.concatenate(dcs, 0).T)

    e1, d_gain_self, d_shift_self = norm_back(e2 + pair_sum(nt(dc, cq)), n1, r1, gain_self)
    z = low(e1)

    do = heads(low(nt(z, wo)))
    eps = jnp.sum(do.astype(F32) * o_full, -1, keepdims=True)
    dp = jnp.einsum("bhqd,bhkd->bhqk", do, v, preferred_element_type=F32)
    ds = low(probs * (dp - eps) * SCALE)
    dq = joined(low(jnp.einsum("bhqk,bhkd->bhqd", ds, k, preferred_element_type=F32)))
    dk = joined(low(jnp.einsum("bhqk,bhqd->bhkd", ds, q, preferred_element_type=F32)))
    dv = joined(low(jnp.einsum("bhqk,bhqd->bhkd", low_probs, do, preferred_element_type=F32)))
    d_tok = pair_sum(nt(dq, wq) + nt(dk, wk) + nt(dv, wv))[:128] + e1[:128]

    vectors = jnp.where(
        first,
        jnp.stack([d_gain_self, d_gain_cross, d_gain_ffn]),
        jnp.stack([d_shift_self, d_shift_cross, d_shift_ffn]),
    )
    zero_bias = jnp.zeros_like(d_bias)
    bias_all = in_order(d_bias, zero_bias, 0).reshape(64, 12, 4)
    small = jnp.concatenate([vectors.reshape(3, 64, 12).transpose(1, 2, 0), bias_all], 2)
    small = jnp.pad(small.transpose(1, 0, 2), ((0, 0), (0, 0), (0, 121)))
    small = small.reshape(12, 4, 4, 4, 128).transpose(0, 3, 1, 2, 4).reshape(12, 64, 128)

    late = []
    late.append(jnp.concatenate([weight_grad(tok, dq, 0), weight_grad(low1, dc, 0)], 2))
    late.append(jnp.concatenate([weight_grad(tok, dk, 1), weight_grad(o_all, columns(z), 1)], 2))
    late.append(jnp.concatenate([weight_grad(tok, dv, 2), low(small)], 2))
    late = [scatter_all(a, 1, order) for a, order in zip(late, ORDERS)]

    def finish(a, n):
        mine, theirs = a.reshape(2, n, a.shape[-1]), None
        theirs = swap(lax.dynamic_index_in_dim(mine, 1 - core, 0, False))
        return lax.dynamic_index_in_dim(mine, core, 0, False), theirs

    wide = jnp.concatenate([a[:, 0] for a in late] + [gr_co[:, 0], gr_in[:, 0]], 1)
    mine, theirs = finish(wide, 6)

    def take(start, size):
        return in_order(mine[:, start : start + size], theirs[:, start : start + size], 1)

    d_wq, d_cq, d_wk, d_wo, d_wv = (take(s, 384) for s in (0, 384, 768, 1152, 1536))
    d_co, d_fi = take(2048, 384), take(2432, 1536)
    s_mine, s_theirs = mine[:, 1920:2048], theirs[:, 1920:2048]
    gains = jnp.where(first, s_mine[:, :3], s_theirs[:, :3])
    shifts = jnp.where(first, s_theirs[:, :3], s_mine[:, :3])
    d_fb = (s_mine[:, 3:7] + s_theirs[:, 3:7]).reshape(24)
    out_mine, out_theirs = finish(gr_out[0, 0, 0] if gr_out.ndim == 5 else gr_out, 24)
    d_fo = in_order(out_mine, out_theirs, 1)
    store = jnp.concatenate(store_grads, 1).reshape(128, 3, 2, 128)
    store = store.transpose(0, 2, 1, 3).reshape(128, 768)
    st_mine, st_theirs = finish(store, 64)
    d_keys = in_order(st_mine[:, :384], st_theirs[:, :384], 1)
    d_values = in_order(st_mine[:, 384:], st_theirs[:, 384:], 1)
    return (
        out[:128], d_tok, d_keys, d_values, d_wq, d_wk, d_wv, d_wo, d_cq, d_co, d_fi, d_fb, d_fo,
        gains[:, 0], shifts[:, 0], gains[:, 1], shifts[:, 1], gains[:, 2], shifts[:, 2],
    )


def solution(mesh):
    grid = Mesh(mesh.devices.reshape(4, 4, 4, 2), ALL)
    split, line, whole = P(ALL, None), P(ALL), P()
    return jax.shard_map(
        shards,
        mesh=grid,
        in_specs=(split,) * 4 + (line,) + (whole,) * 15 + (split,),
        out_specs=(split,) * 11 + (line,) + (split,) + (line,) * 6,
        check_vma=False,
    )
```

time: 1960 us -> 633 us (0.32)
  local copies, waits for them, and re-layouts: 880 us -> 69.6 us
  blocking collectives: 411 us -> 0 us
  starting transfers between devices: 362 us -> 142 us
  matrix products: 235 us -> 42.7 us
  waiting for transfers between devices: 8.9 us -> 159 us
  Pallas kernels: 0 us -> 126 us
  other arithmetic: 22.5 us -> 65.3 us
    unnamed x528 -> x273, local copies, waits for them, and re-layouts: 752 us -> 13.6 us
    unnamed x2 -> x0, blocking collectives: 411 us -> none
    unnamed x129 -> x0, starting transfers between devices: 362 us -> none
    dot_general x77 -> x29, matrix products: 233 us -> 41.3 us  [the longest x8 17.1 us: tn(): lax.dot_general(a, b, (((0,), (0,)), ((), ())), preferred_element_type=F32)]
    ppermute x0 -> x98, starting transfers between devices: none -> 142 us  [the longest x81 139 us: shift_by(): return lax.ppermute(v, axis, [(i, (i + d) % 4) for i in range(4)])]
    pallas_call x0 -> x5, Pallas kernels: none -> 126 us  [the longest x3 54.9 us: cross_bwd(): pl.pallas_call(functools.partial(bwd_body, part=part), grid_spec=pltpu.Pr...]
    ppermute x0 -> x98, waiting for transfers between devices: none -> 106 us  [the longest x81 103 us: shift_by(): return lax.ppermute(v, axis, [(i, (i + d) % 4) for i in range(4)])]
    all_gather x2 -> x1, waiting for transfers between devices: 0.02 us -> 52.8 us  [shards(): kv = lax.all_gather(kv_chip, CHIP, axis=0, tiled=True)]
  transfers between devices with their start and end apart: 134 -> 99, of which waited for: 7 -> 30; matrix products, arithmetic and copies ran while one was open for 65% -> 24% of each run, Pallas kernels for 0% -> 20%
where the time goes in v1:
time: 633 us; the launch traced here: 621 us
  waiting for transfers between devices  159 us (25%)
  starting transfers between devices  142 us (22%)
  Pallas kernels  126 us (20%)
  local copies, waits for them, and re-layouts  69.6 us (11%)
  other arithmetic  65.3 us (10%)
  matrix products  42.7 us (7%)
  between operations  17.4 us (3%)
    ppermute x81, starting transfers between devices, shift_by(): return lax.ppermute(v, axis, [(i, (i + d) % 4) for i in range(4)])  139 us
    ppermute x81, waiting for transfers between devices, shift_by(): return lax.ppermute(v, axis, [(i, (i + d) % 4) for i in range(4)])  103 us
    pallas_call x3, Pallas kernels, cross_bwd(): pl.pallas_call(functools.partial(bwd_body, part=part), grid_spec=pltpu.Pr...  54.9 us
    all_gather x1, waiting for transfers between devices, shards(): kv = lax.all_gather(kv_chip, CHIP, axis=0, tiled=True)  52.8 us
    pallas_call x1, Pallas kernels, cross_fwd(): pl.pallas_call(functools.partial(fwd_body, sub=sub), grid=(3, nb), in_spe...  46.1 us
    pallas_call x1, Pallas kernels, make_mask(): pl.pallas_call(mask_body, out_shape=jax.ShapeDtypeStruct((64, 128, 128),...  24.5 us
    convert_element_type x24, other arithmetic, low(): return v.astype(BF)  24 us
    dot_general x8, matrix products, tn(): lax.dot_general(a, b, (((0,), (0,)), ((), ())), preferred_element_type=F32)  17.1 us
  transfers between devices with their start and end apart: 99, of which 30 were waited for; matrix products, arithmetic and copies ran while one was open for 24% of the time, Pallas kernels for 20%

profile of v1, /device:TPU:8, one launch (start us, length us, event | category | flops | bytes accessed | tf_op | source)
XLA Modules:
  0.0 621.1 jit_solution(15645893404758260608)
XLA Ops:
  11.1 24.5 %mask.1.b0_ref = f32[64,128,128]{2,1,0:T(8,128)} custom-call(s32[128,1024]{1,0:T(8,128)S(1)} %copy-done.2), custom_call_target="tpu_custom_call" | custom-call | tf_op jit(solution)/shard_map/mask/pallas_call | solution.py:56
  52.2 52.8 %all-gather.2.cloned.1.call-done = bf16[8192,768]{1,0:T(8,128)(2,1)} async-done(((bf16[128,768]{1,0:T(8,128)(2,1)}), bf16[8192,768]{1,0:T(8,128)(2,1)}) %all-gather.2.cloned.1.call-update) | async-done | bytes 12582928 | tf_op jit(solution)/shard_map/all_gather | solution.py:262
  105.0 46.1 %cross_fwd.1 = (f32[256,384]{1,0:T(8,128)}, f32[3,2,1,256]{3,2,1,0:T(1,128)}) custom-call(bf16[64,128,768]{2,1,0:T(8,128)(2,1)} %bitcast.209, bf16[64,128,768]{2,1,0:T(8,128)(2,1)} %bitcast.210, f32[64,128,128]{2,1,0:T(8,128)} %mask.1.b0_ref, f32[64,128,128]{2,1,0:T(8,128)} %collective-permute-done.4.b1_ref, bf16[3,2,128,256]{3,2,1,0:T(8,128)(2,1)} %copy.296.ct_ref), custom_call_target="tpu_custom_call" | custom-call | tf_op jit(solution)/shard_map/cross_fwd/pallas_call | solution.py:99
  165.2 7.0 %multiply_convert_fusion = (bf16[256,1536]{1,0:T(8,128)(2,1)S(1)}, f32[256,1536]{1,0:T(8,128)}, f32[256,1536]{1,0:T(8,128)}) fusion(f32[1536]{0:T(1024)S(1)} %copy-done.107, bf16[768,3072]{1,0:T(8,128)(2,1)} %param.32, s32[]{:T(128)S(6)} %select_n.501, f32[256,768]{1,0:T(8,128)S(1)} %get-tuple-element.82, f32[768]{0:T(1024)S(1)} %copy-done.110, ...), kind=kOutput, calls=%fused_computation.38 | convolution fusion | flops 630915072 | bytes 7092228 | tf_op jit(solution)/shard_map/dot_general | solution.py:26
  201.9 4.2 convolution_convert_fusion.1
  214.3 3.6 fusion.12
  220.5 4.8 collective-permute-done.89
  228.6 13.7 %collective-permute-start.93 = (bf16[4,1,1,48,384]{4,3,2,1,0:T(8,128)(2,1)S(1)}, bf16[4,1,1,48,384]{4,3,2,1,0:T(8,128)(2,1)S(1)}, u32[]{:S(2)}, u32[]{:S(2)}) collective-permute-start(bf16[4,1,1,48,384]{4,3,2,1,0:T(8,128)(2,1)S(1)} %get-tuple-element.124), channel_id=1, source_target_pairs={{0,6},{2,0},{4,2},{6,4},{1,7},{3,1},{5,3},{7,5},{8,14},{10,8},{12,... | collective-permute-start | bytes 442376 | tf_op jit(solution)/shard_map/ppermute | solution.py:185
  259.7 3.6 collective-permute-done.84
  286.8 18.2 %cross_bwd1.1 = (bf16[16,128,256]{2,1,0:T(8,128)(2,1)}, bf16[16,128,256]{2,1,0:T(8,128)(2,1)}, bf16[16,128,256]{2,1,0:T(8,128)(2,1)}, bf16[16,128,256]{2,1,0:T(8,128)(2,1)}, f32[128,256]{1,0:T(8,128)}) custom-call(s32[1]{0:T(128)} %bitcast.30.me_ref, bf16[4,4,4,128,768]{4,3,2,1,0:T(8,128)(2,1)} %bitcast.211, bf16[4,4,4,128,768]{4,3,2,1,0:T(8,128)(2,1)} %bitcast.212, ...), custom_call_target="tpu_custom_call" | custom-call | tf_op jit(solution)/shard_map/cross_bwd1/pallas_call | solution.py:152
  305.9 18.4 %cross_bwd0.1 = (bf16[16,128,256]{2,1,0:T(8,128)(2,1)}, bf16[16,128,256]{2,1,0:T(8,128)(2,1)}, bf16[16,128,256]{2,1,0:T(8,128)(2,1)}, bf16[16,128,256]{2,1,0:T(8,128)(2,1)}, f32[128,256]{1,0:T(8,128)}) custom-call(s32[1]{0:T(128)} %bitcast.10.me_ref, bf16[4,4,4,128,768]{4,3,2,1,0:T(8,128)(2,1)} %bitcast.213, bf16[4,4,4,128,768]{4,3,2,1,0:T(8,128)(2,1)} %bitcast.214, ...), custom_call_target="tpu_custom_call" | custom-call | tf_op jit(solution)/shard_map/cross_bwd0/pallas_call | solution.py:152
  325.2 18.3 %cross_bwd2.1 = (bf16[16,128,256]{2,1,0:T(8,128)(2,1)}, bf16[16,128,256]{2,1,0:T(8,128)(2,1)}, bf16[16,128,256]{2,1,0:T(8,128)(2,1)}, bf16[16,128,256]{2,1,0:T(8,128)(2,1)}, f32[128,256]{1,0:T(8,128)}) custom-call(s32[1]{0:T(128)} %bitcast.37.me_ref, bf16[4,4,4,128,768]{4,3,2,1,0:T(8,128)(2,1)} %bitcast.215, bf16[4,4,4,128,768]{4,3,2,1,0:T(8,128)(2,1)} %bitcast.216, ...), custom_call_target="tpu_custom_call" | custom-call | tf_op jit(solution)/shard_map/cross_bwd2/pallas_call | solution.py:152
  364.5 16.9 %collective-permute-done.74 = bf16[12,1,384]{2,0,1:T(8,128)(2,1)S(1)} collective-permute-done((bf16[12,1,384]{2,0,1:T(8,128)(2,1)S(1)}, bf16[12,1,384]{2,0,1:T(8,128)(2,1)S(1)}, u32[]{:S(2)}, u32[]{:S(2)}) %collective-permute-start.74) | collective-permute-done | bytes 9248 | tf_op jit(solution)/shard_map/ppermute | solution.py:185
  381.4 3.8 collective-permute-start.21
  434.0 11.2 %collective-permute-done.66 = bf16[12,1,512]{2,0,1:T(8,128)(2,1)} collective-permute-done((bf16[12,1,512]{2,0,1:T(8,128)(2,1)S(1)}, bf16[12,1,512]{2,0,1:T(8,128)(2,1)}, u32[]{:S(2)}, u32[]{:S(2)}) %collective-permute-start.66) | collective-permute-done | bytes 12320 | tf_op jit(solution)/shard_map/ppermute | solution.py:185
  465.9 6.3 %collective-permute-done.30 = bf16[16,128,256]{2,1,0:T(8,128)(2,1)} collective-permute-done((bf16[16,128,256]{2,1,0:T(8,128)(2,1)}, bf16[16,128,256]{2,1,0:T(8,128)(2,1)}, u32[]{:S(2)}, u32[]{:S(2)}) %collective-permute-start.30) | collective-permute-done | bytes 1048608 | tf_op jit(solution)/shard_map/ppermute | solution.py:185
  472.2 21.3 %collective-permute-done.31 = bf16[16,128,256]{2,1,0:T(8,128)(2,1)} collective-permute-done((bf16[16,128,256]{2,1,0:T(8,128)(2,1)}, bf16[16,128,256]{2,1,0:T(8,128)(2,1)}, u32[]{:S(2)}, u32[]{:S(2)}) %collective-permute-start.31) | collective-permute-done | bytes 1048608 | tf_op jit(solution)/shard_map/ppermute | solution.py:185
  499.2 3.3 collective-permute-start.50
  519.9 4.6 collective-permute-done.41
  534.9 3.8 collective-permute-start.55
  539.5 4.3 collective-permute-start.56
  577.1 7.8 %collective-permute-done.34 = bf16[1,4,128,256]{3,2,1,0:T(8,128)(2,1)S(1)} collective-permute-done((bf16[1,4,128,256]{3,2,1,0:T(8,128)(2,1)}, bf16[1,4,128,256]{3,2,1,0:T(8,128)(2,1)S(1)}, u32[]{:S(2)}, u32[]{:S(2)}) %collective-permute-start.34) | collective-permute-done | bytes 262176 | tf_op jit(solution)/shard_map/ppermute | solution.py:185
  589.8 3.5 collective-permute-start.27
  603.8 3.3 collective-permute-done.18
  (684 shorter events, 298.3 us)
Async XLA Ops:
  7.2 97.8 %all-gather.2.cloned.1.call-start = ((), (), s32[]{:S(2)}) async-start(), calls=%async_computation | async-start | bytes 12779520 | tf_op jit(solution)/shard_map/all_gather | solution.py:262
  10.5 26.0 %collective-permute-start.1 = (s32[1]{0:T(128)}, s32[1]{0:T(128)}, u32[]{:S(2)}, u32[]{:S(2)}) collective-permute-start(s32[1]{0:T(128)} %param.25), channel_id=1, source_target_pairs={{0,1},{1,0},{2,3},{3,2},{4,5},{5,4},{6,7},{7,6},{8,9},{9,8},{10,11... | collective-permute-start | bytes 20 | tf_op jit(solution)/shard_map/ppermute | solution.py:181
  10.7 27.4 %collective-permute-start = (bf16[128,768]{1,0:T(8,128)(2,1)}, bf16[128,768]{1,0:T(8,128)(2,1)S(1)}, u32[]{:S(2)}, u32[]{:S(2)}) collective-permute-start(bf16[128,768]{1,0:T(8,128)(2,1)} %param.21), channel_id=1, source_target_pairs={{0,1},{1,0},{2,3},{3,2},{4,5},{5,4},{6,7},{7,6},{8,9},{9,8},{10,11... | collective-permute-start | bytes 589832 | tf_op jit(solution)/shard_map/ppermute | solution.py:181
  45.4 112.4 %collective-permute-start.7 = (f32[128,768]{1,0:T(8,128)}, f32[128,768]{1,0:T(8,128)}, u32[]{:S(2)}, u32[]{:S(2)}) collective-permute-start(f32[128,768]{1,0:T(8,128)} %param.41), channel_id=1, source_target_pairs={{0,1},{1,0},{2,3},{3,2},{4,5},{5,4},{6,7},{7,6},{8,9},{9,8},{10,11... | collective-permute-start | bytes 1179656 | tf_op jit(solution)/shard_map/ppermute | solution.py:181
  196.5 24.0 %collective-permute-start.90 = (bf16[4,1,4,48,384]{4,3,2,1,0:T(8,128)(2,1)}, bf16[4,1,4,48,384]{4,3,2,1,0:T(8,128)(2,1)}, u32[]{:S(2)}, u32[]{:S(2)}) collective-permute-start(bf16[4,1,4,48,384]{4,3,2,1,0:T(8,128)(2,1)} %get-tuple-element.86), channel_id=1, source_target_pairs={{0,24},{8,0},{16,8},{24,16},{1,25},{9,1},{17,9},{25,17},{2,26},{10... | collective-permute-start | bytes 1769480 | tf_op jit(solution)/shard_map/ppermute | solution.py:185
  197.1 28.2 %collective-permute-start.89 = (bf16[4,1,4,48,384]{4,3,2,1,0:T(8,128)(2,1)}, bf16[4,1,4,48,384]{4,3,2,1,0:T(8,128)(2,1)}, u32[]{:S(2)}, u32[]{:S(2)}) collective-permute-start(bf16[4,1,4,48,384]{4,3,2,1,0:T(8,128)(2,1)} %get-tuple-element.87), channel_id=1, source_target_pairs={{0,16},{8,24},{16,0},{24,8},{1,17},{9,25},{17,1},{25,9},{2,18},{10... | collective-permute-start | bytes 1769480 | tf_op jit(solution)/shard_map/ppermute | solution.py:185
  212.4 29.9 %collective-permute-start.79 = (bf16[12,16,1536]{2,1,0:T(8,128)(2,1)}, bf16[12,16,1536]{2,1,0:T(8,128)(2,1)S(1)}, u32[]{:S(2)}, u32[]{:S(2)}) collective-permute-start(bf16[12,16,1536]{2,1,0:T(8,128)(2,1)} %get-tuple-element.89), channel_id=1, source_target_pairs={{0,96},{32,0},{64,32},{96,64},{1,97},{33,1},{65,33},{97,65},{2,98}... | collective-permute-start | bytes 1769480 | tf_op jit(solution)/shard_map/ppermute | solution.py:185
  218.0 25.0 %collective-permute-start.78 = (bf16[12,16,1536]{2,1,0:T(8,128)(2,1)S(1)}, bf16[12,16,1536]{2,1,0:T(8,128)(2,1)S(1)}, u32[]{:S(2)}, u32[]{:S(2)}) collective-permute-start(bf16[12,16,1536]{2,1,0:T(8,128)(2,1)S(1)} %copy-done.57), channel_id=1, source_target_pairs={{0,64},{32,96},{64,0},{96,32},{1,65},{33,97},{65,1},{97,33},{2,66}... | collective-permute-start | bytes 1769480 | tf_op jit(solution)/shard_map/ppermute | solution.py:185
  220.5 45.3 %collective-permute-start.8 = (f32[256,768]{1,0:T(8,128)}, f32[256,768]{1,0:T(8,128)}, u32[]{:S(2)}, u32[]{:S(2)}) collective-permute-start(f32[256,768]{1,0:T(8,128)} %fusion.12), channel_id=1, source_target_pairs={{0,1},{1,0},{2,3},{3,2},{4,5},{5,4},{6,7},{7,6},{8,9},{9,8},{10,11... | collective-permute-start | bytes 2359304 | tf_op jit(solution)/shard_map/ppermute | solution.py:181
  259.6 101.9 %collective-permute-start.97 = (f32[24,384]{1,0:T(8,128)}, f32[24,384]{1,0:T(8,128)}, u32[]{:S(2)}, u32[]{:S(2)}) collective-permute-start(f32[24,384]{1,0:T(8,128)} %get-tuple-element.221), channel_id=1, source_target_pairs={{0,1},{1,0},{2,3},{3,2},{4,5},{5,4},{6,7},{7,6},{8,9},{9,8},{10,11... | collective-permute-start | bytes 110600 | tf_op jit(solution)/shard_map/ppermute | solution.py:181
  278.3 67.4 %collective-permute-start.70 = (bf16[12,16,384]{2,0,1:T(8,128)(2,1)}, bf16[12,16,384]{2,0,1:T(8,128)(2,1)S(1)}, u32[]{:S(2)}, u32[]{:S(2)}) collective-permute-start(bf16[12,16,384]{2,0,1:T(8,128)(2,1)} %copy.350), channel_id=1, source_target_pairs={{0,6},{2,0},{4,2},{6,4},{1,7},{3,1},{5,3},{7,5},{8,14},{10,8},{12,... | collective-permute-start | bytes 442376 | tf_op jit(solution)/shard_map/ppermute | solution.py:185
  280.2 65.4 %collective-permute-start.68 = (bf16[12,16,384]{2,0,1:T(8,128)(2,1)}, bf16[12,16,384]{2,0,1:T(8,128)(2,1)}, u32[]{:S(2)}, u32[]{:S(2)}) collective-permute-start(bf16[12,16,384]{2,0,1:T(8,128)(2,1)} %copy.348), channel_id=1, source_target_pairs={{0,2},{2,4},{4,6},{6,0},{1,3},{3,5},{5,7},{7,1},{8,10},{10,12},{12... | collective-permute-start | bytes 442376 | tf_op jit(solution)/shard_map/ppermute | solution.py:185
  280.3 65.4 %collective-permute-start.69 = (bf16[12,16,384]{2,0,1:T(8,128)(2,1)}, bf16[12,16,384]{2,0,1:T(8,128)(2,1)}, u32[]{:S(2)}, u32[]{:S(2)}) collective-permute-start(bf16[12,16,384]{2,0,1:T(8,128)(2,1)} %copy.349), channel_id=1, source_target_pairs={{0,4},{2,6},{4,0},{6,2},{1,5},{3,7},{5,1},{7,3},{8,12},{10,14},{12... | collective-permute-start | bytes 442376 | tf_op jit(solution)/shard_map/ppermute | solution.py:185
  345.5 40.4 %collective-permute-start.9 = (f32[256,768]{1,0:T(8,128)S(1)}, f32[256,768]{1,0:T(8,128)S(1)}, u32[]{:S(2)}, u32[]{:S(2)}) collective-permute-start(f32[256,768]{1,0:T(8,128)S(1)} %fusion.73), channel_id=1, source_target_pairs={{0,1},{1,0},{2,3},{3,2},{4,5},{5,4},{6,7},{7,6},{8,9},{9,8},{10,11... | collective-permute-start | bytes 2359304 | tf_op jit(solution)/shard_map/ppermute | solution.py:181
  355.5 96.6 %collective-permute-start.20 = (bf16[16,128,256]{2,1,0:T(8,128)(2,1)}, bf16[16,128,256]{2,1,0:T(8,128)(2,1)}, u32[]{:S(2)}, u32[]{:S(2)}) collective-permute-start(bf16[16,128,256]{2,1,0:T(8,128)(2,1)} %get-tuple-element.46), channel_id=1, source_target_pairs={{0,8},{8,16},{16,24},{24,0},{1,9},{9,17},{17,25},{25,1},{2,10},{10... | collective-permute-start | bytes 3145736 | tf_op jit(solution)/shard_map/ppermute | solution.py:185
  381.4 74.7 %collective-permute-start.21 = (bf16[16,128,256]{2,1,0:T(8,128)(2,1)}, bf16[16,128,256]{2,1,0:T(8,128)(2,1)}, u32[]{:S(2)}, u32[]{:S(2)}) collective-permute-start(bf16[16,128,256]{2,1,0:T(8,128)(2,1)} %get-tuple-element.47), channel_id=1, source_target_pairs={{0,16},{8,24},{16,0},{24,8},{1,17},{9,25},{17,1},{25,9},{2,18},{10... | collective-permute-start | bytes 3145736 | tf_op jit(solution)/shard_map/ppermute | solution.py:185
  422.8 33.7 %collective-permute-start.22 = (bf16[16,128,256]{2,1,0:T(8,128)(2,1)}, bf16[16,128,256]{2,1,0:T(8,128)(2,1)}, u32[]{:S(2)}, u32[]{:S(2)}) collective-permute-start(bf16[16,128,256]{2,1,0:T(8,128)(2,1)} %get-tuple-element.48), channel_id=1, source_target_pairs={{0,24},{8,0},{16,8},{24,16},{1,25},{9,1},{17,9},{25,17},{2,26},{10... | collective-permute-start | bytes 3145736 | tf_op jit(solution)/shard_map/ppermute | solution.py:185
  423.6 35.3 %collective-permute-start.29 = (bf16[16,128,256]{2,1,0:T(8,128)(2,1)}, bf16[16,128,256]{2,1,0:T(8,128)(2,1)}, u32[]{:S(2)}, u32[]{:S(2)}) collective-permute-start(bf16[16,128,256]{2,1,0:T(8,128)(2,1)} %get-tuple-element.50), channel_id=1, source_target_pairs={{0,2},{2,4},{4,6},{6,0},{1,3},{3,5},{5,7},{7,1},{8,10},{10,12},{12... | collective-permute-start | bytes 3145736 | tf_op jit(solution)/shard_map/ppermute | solution.py:185
  452.1 41.5 %collective-permute-start.31 = (bf16[16,128,256]{2,1,0:T(8,128)(2,1)}, bf16[16,128,256]{2,1,0:T(8,128)(2,1)}, u32[]{:S(2)}, u32[]{:S(2)}) collective-permute-start(bf16[16,128,256]{2,1,0:T(8,128)(2,1)} %get-tuple-element.52), channel_id=1, source_target_pairs={{0,6},{2,0},{4,2},{6,4},{1,7},{3,1},{5,3},{7,5},{8,14},{10,8},{12,... | collective-permute-start | bytes 3145736 | tf_op jit(solution)/shard_map/ppermute | solution.py:185
  456.2 41.0 %collective-permute-start.11 = (bf16[16,128,256]{2,1,0:T(8,128)(2,1)}, bf16[16,128,256]{2,1,0:T(8,128)(2,1)}, u32[]{:S(2)}, u32[]{:S(2)}) collective-permute-start(bf16[16,128,256]{2,1,0:T(8,128)(2,1)} %get-tuple-element.42), channel_id=1, source_target_pairs={{0,32},{32,64},{64,96},{96,0},{1,33},{33,65},{65,97},{97,1},{2,34}... | collective-permute-start | bytes 3145736 | tf_op jit(solution)/shard_map/ppermute | solution.py:185
  456.6 42.6 %collective-permute-start.12 = (bf16[16,128,256]{2,1,0:T(8,128)(2,1)}, bf16[16,128,256]{2,1,0:T(8,128)(2,1)}, u32[]{:S(2)}, u32[]{:S(2)}) collective-permute-start(bf16[16,128,256]{2,1,0:T(8,128)(2,1)} %get-tuple-element.43), channel_id=1, source_target_pairs={{0,64},{32,96},{64,0},{96,32},{1,65},{33,97},{65,1},{97,33},{2,66}... | collective-permute-start | bytes 3145736 | tf_op jit(solution)/shard_map/ppermute | solution.py:185
  458.9 43.6 %collective-permute-start.13 = (bf16[16,128,256]{2,1,0:T(8,128)(2,1)}, bf16[16,128,256]{2,1,0:T(8,128)(2,1)}, u32[]{:S(2)}, u32[]{:S(2)}) collective-permute-start(bf16[16,128,256]{2,1,0:T(8,128)(2,1)} %get-tuple-element.44), channel_id=1, source_target_pairs={{0,96},{32,0},{64,32},{96,64},{1,97},{33,1},{65,33},{97,65},{2,98}... | collective-permute-start | bytes 3145736 | tf_op jit(solution)/shard_map/ppermute | solution.py:185
  472.2 138.6 %collective-permute-start.10 = (f32[256,768]{1,0:T(8,128)}, f32[256,768]{1,0:T(8,128)}, u32[]{:S(2)}, u32[]{:S(2)}) collective-permute-start(f32[256,768]{1,0:T(8,128)} %convolution_add_fusion.1), channel_id=1, source_target_pairs={{0,1},{1,0},{2,3},{3,2},{4,5},{5,4},{6,7},{7,6},{8,9},{9,8},{10,11... | collective-permute-start | bytes 2359304 | tf_op jit(solution)/shard_map/ppermute | solution.py:181
  516.3 54.6 %collective-permute-start.23 = (bf16[1,4,128,256]{3,2,1,0:T(8,128)(2,1)}, bf16[1,4,128,256]{3,2,1,0:T(8,128)(2,1)}, u32[]{:S(2)}, u32[]{:S(2)}) collective-permute-start(bf16[1,4,128,256]{3,2,1,0:T(8,128)(2,1)} %get-tuple-element.103), channel_id=1, source_target_pairs={{0,2},{2,4},{4,6},{6,0},{1,3},{3,5},{5,7},{7,1},{8,10},{10,12},{12... | collective-permute-start | bytes 786440 | tf_op jit(solution)/shard_map/ppermute | solution.py:185
  (203 other events, 2075.9 us)
Sparse Core Ops, SparseCore 0:
  11.5 93.5 all-gather.1
